TPU v7x, 128 devices: a whole 4x4x4 slice. The times are simulated.
128 devices in a mesh: dp: 4 (over z), ctx: 8 (over y, core), tensor: 4 (over x).
Axes of the slice: x: 4, y: 4, z: 4, core: 2. Of those that a mesh axis runs over, the one named last changes fastest.
Arguments:
- queries: bfloat16 [16384, 64, 128], P(('dp', 'ctx', 'tensor')), parts along dimension 0, may hold values from -8 to 8
- key_states: bfloat16 [16384, 8, 128], P(('dp', 'ctx', 'tensor')), parts along dimension 0, may hold values from -8 to 8
- value_states: bfloat16 [16384, 8, 128], P(('dp', 'ctx', 'tensor')), parts along dimension 0, may hold values from -6 to 6
- grad_out: bfloat16 [16384, 64, 128], P(('dp', 'ctx', 'tensor')), parts along dimension 0, may hold values from -6 to 6
- doc_lengths: int32 [36], P('dp'), parts along dimension 0, may hold values from 4 to 1024, as said below
Outputs:
- attended: bfloat16 [16384, 64, 128], P(('dp', 'ctx', 'tensor')), parts along dimension 0
- grad_queries: bfloat16 [16384, 64, 128], P(('dp', 'ctx', 'tensor')), parts along dimension 0
- grad_keys: bfloat16 [16384, 8, 128], P(('dp', 'ctx', 'tensor')), parts along dimension 0
- grad_values: bfloat16 [16384, 8, 128], P(('dp', 'ctx', 'tensor')), parts along dimension 0
There are 4 independent parts, one for each index of `dp`. A program takes and returns all parts, laid end to end along the dimension named above; each array names one. Nothing has to cross between parts.
Inputs may be any that keep to these rules, and one draw needn't show every extreme that they name: `doc_lengths`: 9 lengths adding up to 4096; one document has exactly 1024 tokens; the others form pairs whose lengths add up to 768.
All inputs are finite; a program needn't handle non-finite values.
Results may differ from a plain program's by a relative error of at most 0.039.
Values may be sent and summed in bfloat16 or wider, within the bound.
No kernel may reach another device: no remote copies, remote signals or barrier semaphores. Data moves between devices by JAX's collectives and lax.ppermute only.
A program may use at most 192 MiB of HBM per device.

v0:
```python
import math

import jax
import jax.numpy as jnp
from jax import lax
from jax.sharding import PartitionSpec as P


def contract(left, right, dims):
    return lax.dot_general(left, right, (dims, ((), ())), preferred_element_type=jnp.float32)


def group_pass(query_heads, grad_heads, key_rows, value_rows, segment):
    seq_total, head_count, head_width = query_heads.shape
    scale = head_width ** (-0.5)
    block_rows = math.gcd(seq_total, 512)
    window = block_rows + seq_total // 4
    positions = jnp.arange(seq_total, dtype=jnp.int32)
    key_grad = jnp.zeros((seq_total, head_width), jnp.float32)
    value_grad = jnp.zeros((seq_total, head_width), jnp.float32)
    out_blocks = []
    grad_blocks = []
    for block_index in range(seq_total // block_rows):
        start_row = block_index * block_rows
        stop_row = start_row + block_rows
        key_low = max(0, stop_row - window)
        query_block = query_heads[start_row:stop_row].reshape(block_rows * head_count, head_width)
        cotangent = grad_heads[start_row:stop_row].reshape(block_rows * head_count, head_width)
        key_block = key_rows[key_low:stop_row]
        value_block = value_rows[key_low:stop_row]
        query_pos = jnp.repeat(positions[start_row:stop_row], head_count)
        query_seg = jnp.repeat(segment[start_row:stop_row], head_count)
        allowed = (query_seg[:, None] == segment[None, key_low:stop_row]) & (
            positions[None, key_low:stop_row] <= query_pos[:, None]
        )
        scores = contract(query_block, key_block, ((1,), (1,))) * scale
        scores = jnp.where(allowed, scores, -jnp.inf)
        row_max = jnp.max(scores, axis=1)
        exponent = jnp.exp(scores - row_max[:, None])
        totals = jnp.sum(exponent, axis=1)
        attended_block = (
            contract(exponent.astype(jnp.bfloat16), value_block, ((1,), (0,))) / totals[:, None]
        ).astype(jnp.bfloat16)
        probs = exponent / totals[:, None]
        dprobs = contract(cotangent, value_block, ((1,), (1,)))
        delta = jnp.sum(cotangent.astype(jnp.float32) * attended_block.astype(jnp.float32), axis=1)
        dscores = (probs * (dprobs - delta[:, None])).astype(jnp.bfloat16)
        grad_block = (scale * contract(dscores, key_block, ((1,), (0,)))).astype(jnp.bfloat16)
        key_grad = key_grad.at[key_low:stop_row].add(
            scale * contract(dscores, query_block, ((0,), (0,)))
        )
        value_grad = value_grad.at[key_low:stop_row].add(
            contract(probs.astype(jnp.bfloat16), cotangent, ((0,), (0,)))
        )
        out_blocks.append(attended_block.reshape(block_rows, head_count, head_width))
        grad_blocks.append(grad_block.reshape(block_rows, head_count, head_width))
    return (
        jnp.concatenate(out_blocks, axis=0),
        jnp.concatenate(grad_blocks, axis=0),
        key_grad,
        value_grad,
    )


def shards(queries, key_states, value_states, grad_out, doc_lengths):
    tok_rows, head_count, head_width = queries.shape
    kv_count = key_states.shape[1]
    ctx_size = lax.axis_size("ctx")
    tensor_size = lax.axis_size("tensor")
    group_size = ctx_size * tensor_size
    local_heads = head_count // group_size
    slot_repeat = head_count // kv_count // local_heads
    key_slots = jnp.repeat(key_states, slot_repeat, axis=1)
    value_slots = jnp.repeat(value_states, slot_repeat, axis=1)
    seq_total = group_size * tok_rows
    arrived = (
        lax.all_to_all(queries[None], ("ctx", "tensor"), split_axis=2, concat_axis=0, tiled=True),
        lax.all_to_all(grad_out[None], ("ctx", "tensor"), split_axis=2, concat_axis=0, tiled=True),
        lax.all_to_all(key_slots[None], ("ctx", "tensor"), split_axis=2, concat_axis=0, tiled=True),
        lax.all_to_all(
            value_slots[None], ("ctx", "tensor"), split_axis=2, concat_axis=0, tiled=True
        ),
    )
    query_heads, grad_heads, key_heads, value_heads = [
        piece.reshape(seq_total, piece.shape[2], head_width) for piece in arrived
    ]
    positions = jnp.arange(seq_total, dtype=jnp.int32)
    doc_ends = jnp.cumsum(doc_lengths)
    segment = jnp.sum((positions[:, None] >= doc_ends[None, :]).astype(jnp.int32), axis=1)
    attended, grad_block, key_grad, value_grad = group_pass(
        query_heads, grad_heads, key_heads[:, 0], value_heads[:, 0], segment
    )
    returned = (
        lax.all_to_all(
            attended.reshape(group_size, tok_rows, local_heads, head_width),
            ("ctx", "tensor"),
            split_axis=0,
            concat_axis=2,
            tiled=True,
        ),
        lax.all_to_all(
            grad_block.reshape(group_size, tok_rows, local_heads, head_width),
            ("ctx", "tensor"),
            split_axis=0,
            concat_axis=2,
            tiled=True,
        ),
    )
    partials = (
        lax.all_to_all(
            key_grad.reshape(group_size, tok_rows, 1, head_width),
            ("ctx", "tensor"),
            split_axis=0,
            concat_axis=2,
            tiled=True,
        ),
        lax.all_to_all(
            value_grad.reshape(group_size, tok_rows, 1, head_width),
            ("ctx", "tensor"),
            split_axis=0,
            concat_axis=2,
            tiled=True,
        ),
    )
    attended_out = returned[0].reshape(tok_rows, head_count, head_width)
    grad_queries = returned[1].reshape(tok_rows, head_count, head_width)
    grad_keys = (
        partials[0]
        .reshape(tok_rows, kv_count, slot_repeat, head_width)
        .sum(axis=2)
        .astype(jnp.bfloat16)
    )
    grad_values = (
        partials[1]
        .reshape(tok_rows, kv_count, slot_repeat, head_width)
        .sum(axis=2)
        .astype(jnp.bfloat16)
    )
    return (attended_out, grad_queries, grad_keys, grad_values)


def solution(mesh):
    placed = (
        P(("dp", "ctx", "tensor"), None, None),
        P(("dp", "ctx", "tensor"), None, None),
        P(("dp", "ctx", "tensor"), None, None),
        P(("dp", "ctx", "tensor"), None, None),
        P("dp"),
    )
    return jax.shard_map(
        shards,
        mesh=mesh,
        in_specs=placed,
        out_specs=(
            P(("dp", "ctx", "tensor"), None, None),
            P(("dp", "ctx", "tensor"), None, None),
            P(("dp", "ctx", "tensor"), None, None),
            P(("dp", "ctx", "tensor"), None, None),
        ),
        check_vma=False,
    )
```

profile of v0, /device:TPU:105, one launch (start us, length us, event | category | flops | bytes accessed | tf_op | source)
XLA Modules:
  0.0 342.6 jit_solution(459007727435810555)
XLA Ops:
  2.8 7.9 %all-to-all-start.1 = ((bf16[1,128,32,128]{3,1,0,2:T(8,128)(2,1)}), bf16[1,128,32,128]{3,1,0,2:T(8,128)(2,1)S(1)}, u32[]{:S(2)}, u32[]{:S(2)}) async-start(bf16[1,128,32,128]{3,1,0,2:T(8,128)(2,1)} %bitcast.6), calls=%async_computation.1 | async-start | bytes 2097152 | tf_op jit(solution)/shard_map/all_to_all | solution.py:79
  11.7 14.8 %all-to-all-done.1 = bf16[1,128,32,128]{3,1,0,2:T(8,128)(2,1)S(1)} async-done(((bf16[1,128,32,128]{3,1,0,2:T(8,128)(2,1)}), bf16[1,128,32,128]{3,1,0,2:T(8,128)(2,1)S(1)}, u32[]{:S(2)}, u32[]{:S(2)}) %all-to-all-start.1) | async-done | bytes 1048608 | tf_op jit(solution)/shard_map/all_to_all | solution.py:79
  27.7 5.5 %all-to-all-start.2 = ((bf16[1,128,32,128]{3,1,0,2:T(8,128)(2,1)}), bf16[1,128,32,128]{3,1,0,2:T(8,128)(2,1)S(1)}, u32[]{:S(2)}, u32[]{:S(2)}) async-start(bf16[1,128,32,128]{3,1,0,2:T(8,128)(2,1)} %bitcast.10), calls=%async_computation.2 | async-start | bytes 2097152 | tf_op jit(solution)/shard_map/all_to_all | solution.py:80
  33.2 4.3 %copy.75 = bf16[128,64,128]{2,0,1:T(8,128)(2,1)} copy(bf16[128,64,128]{2,1,0:T(8,128)(2,1)} %param.37) | data formatting | bytes 4194304 | tf_op args[0]
  37.5 11.6 %all-to-all-done.2 = bf16[1,128,32,128]{3,1,0,2:T(8,128)(2,1)S(1)} async-done(((bf16[1,128,32,128]{3,1,0,2:T(8,128)(2,1)}), bf16[1,128,32,128]{3,1,0,2:T(8,128)(2,1)S(1)}, u32[]{:S(2)}, u32[]{:S(2)}) %all-to-all-start.2) | async-done | bytes 1048608 | tf_op jit(solution)/shard_map/all_to_all | solution.py:80
  49.0 6.0 %all-to-all-start = ((bf16[1,128,64,128]{3,1,0,2:T(8,128)(2,1)}), bf16[1,128,64,128]{3,1,0,2:T(8,128)(2,1)}, u32[]{:S(2)}, u32[]{:S(2)}) async-start(bf16[1,128,64,128]{3,1,0,2:T(8,128)(2,1)} %bitcast.189), calls=%async_computation | async-start | bytes 4194304 | tf_op jit(solution)/shard_map/all_to_all | solution.py:77
  55.0 4.3 %copy.73 = bf16[128,64,128]{2,0,1:T(8,128)(2,1)} copy(bf16[128,64,128]{2,1,0:T(8,128)(2,1)} %param.40) | data formatting | bytes 4194304 | tf_op args[3]
  59.7 22.0 %all-to-all-done = bf16[1,128,64,128]{3,1,0,2:T(8,128)(2,1)} async-done(((bf16[1,128,64,128]{3,1,0,2:T(8,128)(2,1)}), bf16[1,128,64,128]{3,1,0,2:T(8,128)(2,1)}, u32[]{:S(2)}, u32[]{:S(2)}) %all-to-all-start) | async-done | bytes 2097184 | tf_op jit(solution)/shard_map/all_to_all | solution.py:77
  81.7 6.6 %all-to-all-start.4 = ((bf16[1,128,64,128]{3,1,0,2:T(8,128)(2,1)}), bf16[1,128,64,128]{3,1,0,2:T(8,128)(2,1)}, u32[]{:S(2)}, u32[]{:S(2)}) async-start(bf16[1,128,64,128]{3,1,0,2:T(8,128)(2,1)} %bitcast.188), calls=%async_computation.4 | async-start | bytes 4194304 | tf_op jit(solution)/shard_map/all_to_all | solution.py:78
  112.0 3.8 %copy.74 = bf16[1,128,32,2,128]{4,3,1,2,0:T(2,128)(2,1)S(1)} copy(bf16[1,128,32,2,128]{4,1,3,2,0:T(8,128)(2,1)} %bitcast.3) | data formatting | bytes 4194304 | tf_op jit(solution)/shard_map/all_to_all | solution.py:77
  117.6 4.0 %copy.72 = bf16[1,128,32,2,128]{4,3,1,2,0:T(2,128)(2,1)S(1)} copy(bf16[1,128,32,2,128]{4,1,3,2,0:T(8,128)(2,1)} %bitcast.50) | data formatting | bytes 4194304 | tf_op jit(solution)/shard_map/all_to_all | solution.py:78
  121.6 2.4 fusion.178
  150.6 4.0 %fusion.110 = f32[4096,128]{1,0:T(8,128)S(1)} fusion(f32[4096,128]{1,0:T(8,128)S(1)} %scatter-add.66, bf16[1024,128]{1,0:T(8,128)(2,1)S(1)} %bitcast.268, f32[1024,1024]{0,1:T(8,128)} %copy-done.14, f32[1024]{0:T(1024)S(1)} %fusion.19, f32[1024]{0:T(1024)S(1)} %get-tuple-element.252, f32[512,128]{1,0:T(8,128)S(1)} %copy-done.57), kind=kOutput, calls=%fused_computation.119 | convolution fusion | flops 271712256 | bytes 5251072 | tf_op jit(solution)/shard_map/dot_general | solution.py:10
  154.6 4.6 %fusion.66 = f32[4096,128]{1,0:T(8,128)S(1)} fusion(f32[4096,128]{1,0:T(8,128)S(1)} %fusion.110, bf16[1024,128]{1,0:T(8,128)(2,1)S(1)} %bitcast.264, f32[1024,1536]{1,0:T(8,128)} %copy-done.6, f32[1024]{0:T(1024)S(1)} %fusion.1, f32[1024]{0:T(1024)S(1)} %get-tuple-element.254), kind=kOutput, calls=%fused_computation.85 | convolution fusion | flops 407568384 | bytes 8134656 | tf_op jit(solution)/shard_map/dot_general | solution.py:10
  159.2 2.4 fusion.72
  161.7 2.0 fusion.78
  163.8 2.0 fusion.84
  165.8 2.0 fusion.90
  167.9 2.0 fusion.96
  171.3 7.6 %all-to-all-start.7 = ((f32[32,128,1,128]{3,1,2,0:T(8,128)}), f32[32,128,1,128]{3,1,2,0:T(8,128)S(1)}, u32[]{:S(2)}, u32[]{:S(2)}) async-start(f32[32,128,1,128]{3,1,2,0:T(8,128)} %bitcast.187), calls=%async_computation.7 | async-start | bytes 4194304 | tf_op jit(solution)/shard_map/all_to_all | solution.py:117
  180.4 4.6 %multiply_reduce_fusion.6 = (f32[1024]{0:T(1024)S(1)}, bf16[1024,128]{1,0:T(8,128)(2,1)}) fusion(bf16[1024,128]{1,0:T(8,128)(2,1)} %bitcast.267, f32[1024]{0:T(1024)S(1)} %fusion.19, bf16[1024,128]{1,0:T(8,128)(2,1)} %bitcast.276, f32[1024,1024]{0,1:T(8,128)} %copy-done.14, f32[1024]{0:T(1024)S(1)} %get-tuple-element.252), kind=kOutput, calls=%fused_computation.159 | convolution fusion | flops 271318016 | bytes 4993024 | tf_op jit(solution)/shard_map/dot_general | solution.py:10
  188.5 2.0 multiply_convert_fusion.5
  193.7 3.0 fusion.52
  198.6 2.0 multiply_convert_fusion.4
  202.3 3.1 fusion.54
  207.3 2.2 multiply_convert_fusion.3
  209.6 1.8 multiply_reduce_fusion.2
  211.4 2.0 multiply_convert_fusion.2
  215.6 2.0 multiply_convert_fusion.1
  218.8 3.1 fusion.56
  221.8 3.2 fusion.58
  225.0 3.2 fusion.60
  230.8 2.2 multiply_convert_fusion
  234.8 3.1 fusion.62
  237.9 7.6 %all-to-all-start.6 = ((f32[32,128,1,128]{3,1,2,0:T(8,128)}), f32[32,128,1,128]{3,1,2,0:T(8,128)}, u32[]{:S(2)}, u32[]{:S(2)}) async-start(f32[32,128,1,128]{3,1,2,0:T(8,128)} %bitcast.73), calls=%async_computation.6 | async-start | bytes 4194304 | tf_op jit(solution)/shard_map/all_to_all | solution.py:110
  248.1 2.9 fusion.121
  257.6 14.4 %all-to-all-done.6 = f32[32,128,1,128]{3,1,2,0:T(8,128)} async-done(((f32[32,128,1,128]{3,1,2,0:T(8,128)}), f32[32,128,1,128]{3,1,2,0:T(8,128)}, u32[]{:S(2)}, u32[]{:S(2)}) %all-to-all-start.6) | async-done | bytes 2097184 | tf_op jit(solution)/shard_map/all_to_all | solution.py:110
  272.0 5.9 %all-to-all-start.5 = ((bf16[32,128,2,128]{3,2,1,0:T(2,128)(2,1)}), bf16[32,128,2,128]{3,2,1,0:T(2,128)(2,1)}, u32[]{:S(2)}, u32[]{:S(2)}) async-start(bf16[32,128,2,128]{3,2,1,0:T(2,128)(2,1)} %bitcast.68), calls=%async_computation.5 | async-start | bytes 4194304 | tf_op jit(solution)/shard_map/all_to_all | solution.py:101
  282.3 1.8 constant_dynamic-update-slice_fusion.2
  284.2 1.8 constant_dynamic-update-slice_fusion.1
  286.0 1.8 constant_dynamic-update-slice_fusion
  287.8 16.7 %all-to-all-done.5 = bf16[32,128,2,128]{3,2,1,0:T(2,128)(2,1)} async-done(((bf16[32,128,2,128]{3,2,1,0:T(2,128)(2,1)}), bf16[32,128,2,128]{3,2,1,0:T(2,128)(2,1)}, u32[]{:S(2)}, u32[]{:S(2)}) %all-to-all-start.5) | async-done | bytes 2097184 | tf_op jit(solution)/shard_map/all_to_all | solution.py:101
  304.5 6.4 %all-to-all-start.3 = ((bf16[32,128,2,128]{3,2,1,0:T(2,128)(2,1)}), bf16[32,128,2,128]{3,2,1,0:T(2,128)(2,1)}, u32[]{:S(2)}, u32[]{:S(2)}) async-start(bf16[32,128,2,128]{3,2,1,0:T(2,128)(2,1)} %bitcast.45), calls=%async_computation.3 | async-start | bytes 4194304 | tf_op jit(solution)/shard_map/all_to_all | solution.py:94
  314.5 2.1 copy.59
  316.7 2.7 copy.63
  319.4 17.9 %all-to-all-done.3 = bf16[32,128,2,128]{3,2,1,0:T(2,128)(2,1)} async-done(((bf16[32,128,2,128]{3,2,1,0:T(2,128)(2,1)}), bf16[32,128,2,128]{3,2,1,0:T(2,128)(2,1)}, u32[]{:S(2)}, u32[]{:S(2)}) %all-to-all-start.3) | async-done | bytes 2097184 | tf_op jit(solution)/shard_map/all_to_all | solution.py:94
  337.2 2.1 copy.54
  339.4 2.7 copy.62
  (354 shorter events, 95.8 us)
Async XLA Ops:
  2.8 23.7 %all-to-all-start.1 = ((bf16[1,128,32,128]{3,1,0,2:T(8,128)(2,1)}), bf16[1,128,32,128]{3,1,0,2:T(8,128)(2,1)S(1)}, u32[]{:S(2)}, u32[]{:S(2)}) async-start(bf16[1,128,32,128]{3,1,0,2:T(8,128)(2,1)} %bitcast.6), calls=%async_computation.1 | async-start | bytes 2097152 | tf_op jit(solution)/shard_map/all_to_all | solution.py:79
  27.7 21.3 %all-to-all-start.2 = ((bf16[1,128,32,128]{3,1,0,2:T(8,128)(2,1)}), bf16[1,128,32,128]{3,1,0,2:T(8,128)(2,1)S(1)}, u32[]{:S(2)}, u32[]{:S(2)}) async-start(bf16[1,128,32,128]{3,1,0,2:T(8,128)(2,1)} %bitcast.10), calls=%async_computation.2 | async-start | bytes 2097152 | tf_op jit(solution)/shard_map/all_to_all | solution.py:80
  49.0 10.3 %copy-start.102 = (s32[9]{0:T(128)S(1)}, s32[9]{0:T(128)}, u32[]{:S(2)}) copy-start(s32[9]{0:T(128)} %param.41) | copy-start | bytes 112
  49.0 32.7 %all-to-all-start = ((bf16[1,128,64,128]{3,1,0,2:T(8,128)(2,1)}), bf16[1,128,64,128]{3,1,0,2:T(8,128)(2,1)}, u32[]{:S(2)}, u32[]{:S(2)}) async-start(bf16[1,128,64,128]{3,1,0,2:T(8,128)(2,1)} %bitcast.189), calls=%async_computation | async-start | bytes 4194304 | tf_op jit(solution)/shard_map/all_to_all | solution.py:77
  59.5 35.9 %copy-start.71 = (s32[512]{0:T(512)}, s32[512]{0:T(512)S(1)}, u32[]{:S(2)}) copy-start(s32[512]{0:T(512)S(1)} %iota_add_fusion.14) | copy-start | bytes 6148
  59.6 46.5 %copy-start.23 = (s32[4096]{0:T(1024)}, s32[4096]{0:T(1024)S(1)}, u32[]{:S(2)}) copy-start(s32[4096]{0:T(1024)S(1)} %convert_reduce_fusion) | copy-start | bytes 49156
  59.7 35.8 %copy-start.69 = (s32[512]{0:T(512)}, s32[512]{0:T(512)S(1)}, u32[]{:S(2)}) copy-start(s32[512]{0:T(512)S(1)} %get-tuple-element.243) | copy-start | bytes 6148
  81.7 35.9 %all-to-all-start.4 = ((bf16[1,128,64,128]{3,1,0,2:T(8,128)(2,1)}), bf16[1,128,64,128]{3,1,0,2:T(8,128)(2,1)}, u32[]{:S(2)}, u32[]{:S(2)}) async-start(bf16[1,128,64,128]{3,1,0,2:T(8,128)(2,1)} %bitcast.188), calls=%async_computation.4 | async-start | bytes 4194304 | tf_op jit(solution)/shard_map/all_to_all | solution.py:78
  117.5 12.1 %copy-start.20 = (bf16[4,1,128,2,128]{4,3,2,0,1:T(2,128)(2,1)}, bf16[4,1,128,2,128]{4,3,2,0,1:T(2,128)(2,1)S(1)}, u32[]{:S(2)}) copy-start(bf16[4,1,128,2,128]{4,3,2,0,1:T(2,128)(2,1)S(1)} %get-tuple-element.222) | copy-start | bytes 786436
  117.5 13.9 %copy-start.18 = (bf16[4,1,128,2,128]{4,3,2,0,1:T(2,128)(2,1)}, bf16[4,1,128,2,128]{4,3,2,0,1:T(2,128)(2,1)S(1)}, u32[]{:S(2)}) copy-start(bf16[4,1,128,2,128]{4,3,2,0,1:T(2,128)(2,1)S(1)} %get-tuple-element.221) | copy-start | bytes 786436
  117.5 18.3 %copy-start.16 = (bf16[4,1,128,2,128]{4,3,2,0,1:T(2,128)(2,1)}, bf16[4,1,128,2,128]{4,3,2,0,1:T(2,128)(2,1)S(1)}, u32[]{:S(2)}) copy-start(bf16[4,1,128,2,128]{4,3,2,0,1:T(2,128)(2,1)S(1)} %get-tuple-element.220) | copy-start | bytes 786436
  117.5 6.5 %copy-start.70 = (s32[512]{0:T(512)S(1)}, s32[512]{0:T(512)}, u32[]{:S(2)}) copy-start(s32[512]{0:T(512)} %copy-done.69) | copy-start | bytes 6148
  117.6 6.5 %copy-start.72 = (s32[512]{0:T(512)S(1)}, s32[512]{0:T(512)}, u32[]{:S(2)}) copy-start(s32[512]{0:T(512)} %copy-done.71) | copy-start | bytes 6148
  117.6 6.5 %copy-start.99 = (s32[1024]{0:T(1024)S(1)}, s32[1024]{0:T(1024)}, u32[]{:S(2)}) copy-start(s32[1024]{0:T(1024)} %eq.120) | copy-start | bytes 12292
  117.6 6.5 %copy-start.100 = (s32[1024]{0:T(1024)S(1)}, s32[1024]{0:T(1024)}, u32[]{:S(2)}) copy-start(s32[1024]{0:T(1024)} %le.121) | copy-start | bytes 12292
  124.0 41.8 %copy-start.44 = (bf16[4,1,128,2,128]{4,3,2,0,1:T(2,128)(2,1)}, bf16[4,1,128,2,128]{4,3,2,0,1:T(2,128)(2,1)S(1)}, u32[]{:S(2)}) copy-start(bf16[4,1,128,2,128]{4,3,2,0,1:T(2,128)(2,1)S(1)} %get-tuple-element.209) | copy-start | bytes 786436
  124.0 43.9 %copy-start.42 = (bf16[4,1,128,2,128]{4,3,2,0,1:T(2,128)(2,1)}, bf16[4,1,128,2,128]{4,3,2,0,1:T(2,128)(2,1)S(1)}, u32[]{:S(2)}) copy-start(bf16[4,1,128,2,128]{4,3,2,0,1:T(2,128)(2,1)S(1)} %get-tuple-element.208) | copy-start | bytes 786436
  137.5 21.7 %copy-start.5 = (f32[1024,1536]{1,0:T(8,128)}, f32[1024,1536]{1,0:T(8,128)S(1)}, u32[]{:S(2)}) copy-start(f32[1024,1536]{1,0:T(8,128)S(1)} %get-tuple-element.257) | copy-start | bytes 18874372
  140.4 21.3 %copy-start.4 = (f32[1024,1536]{1,0:T(8,128)}, f32[1024,1536]{1,0:T(8,128)S(1)}, u32[]{:S(2)}) copy-start(f32[1024,1536]{1,0:T(8,128)S(1)} %get-tuple-element.259) | copy-start | bytes 18874372
  143.3 20.4 %copy-start.3 = (f32[1024,1536]{1,0:T(8,128)}, f32[1024,1536]{1,0:T(8,128)S(1)}, u32[]{:S(2)}) copy-start(f32[1024,1536]{1,0:T(8,128)S(1)} %get-tuple-element.261) | copy-start | bytes 18874372
  146.3 19.6 %copy-start.2 = (f32[1024,1536]{1,0:T(8,128)}, f32[1024,1536]{1,0:T(8,128)S(1)}, u32[]{:S(2)}) copy-start(f32[1024,1536]{1,0:T(8,128)S(1)} %get-tuple-element.263) | copy-start | bytes 18874372
  149.2 18.7 %copy-start.1 = (f32[1024,1536]{1,0:T(8,128)}, f32[1024,1536]{1,0:T(8,128)S(1)}, u32[]{:S(2)}) copy-start(f32[1024,1536]{1,0:T(8,128)S(1)} %get-tuple-element.265) | copy-start | bytes 18874372
  154.6 4.6 %copy-start.50 = (bf16[4,1,128,2,128]{4,3,2,0,1:T(2,128)(2,1)S(1)}, bf16[4,1,128,2,128]{4,3,2,0,1:T(2,128)(2,1)}, u32[]{:S(2)}) copy-start(bf16[4,1,128,2,128]{4,3,2,0,1:T(2,128)(2,1)} %get-tuple-element.212) | copy-start | bytes 786436
  171.3 66.6 %all-to-all-start.7 = ((f32[32,128,1,128]{3,1,2,0:T(8,128)}), f32[32,128,1,128]{3,1,2,0:T(8,128)S(1)}, u32[]{:S(2)}, u32[]{:S(2)}) async-start(f32[32,128,1,128]{3,1,2,0:T(8,128)} %bitcast.187), calls=%async_computation.7 | async-start | bytes 4194304 | tf_op jit(solution)/shard_map/all_to_all | solution.py:117
  178.9 6.0 %copy-start.15 = (f32[1024,1024]{0,1:T(8,128)S(1)}, f32[1024,1024]{0,1:T(8,128)}, u32[]{:S(2)}) copy-start(f32[1024,1024]{0,1:T(8,128)} %copy-done.14) | copy-start | bytes 12582916
  178.9 6.0 %copy-start.55 = (bf16[4,1,128,2,128]{4,3,2,0,1:T(2,128)(2,1)S(1)}, bf16[4,1,128,2,128]{4,3,2,0,1:T(2,128)(2,1)}, u32[]{:S(2)}) copy-start(bf16[4,1,128,2,128]{4,3,2,0,1:T(2,128)(2,1)} %get-tuple-element.214) | copy-start | bytes 786436
  178.9 6.0 %copy-start.61 = (bf16[8,1,128,1,128]{4,2,0,3,1:T(8,128)(2,1)S(1)}, bf16[8,1,128,1,128]{4,2,0,3,1:T(8,128)(2,1)}, u32[]{:S(2)}) copy-start(bf16[8,1,128,1,128]{4,2,0,3,1:T(8,128)(2,1)} %slice.650) | copy-start | bytes 786436
  180.4 5.7 %slice-start.10 = ((s8[6291456]{0:T(1024)(128)(4,1)}), s8[4194304]{0:T(1024)(128)(4,1)S(1)}, s32[]{:S(2)}) async-start(s8[6291456]{0:T(1024)(128)(4,1)} %bitcast.204), calls=%async_computation.18 | async-start | bytes 8388608
  190.5 6.3 %slice-start.8 = ((s8[6291456]{0:T(1024)(128)(4,1)}), s8[4194304]{0:T(1024)(128)(4,1)S(1)}, s32[]{:S(2)}) async-start(s8[6291456]{0:T(1024)(128)(4,1)} %bitcast.202), calls=%async_computation.16 | async-start | bytes 8388608
  196.8 8.6 %slice-start.6 = ((s8[6291456]{0:T(1024)(128)(4,1)}), s8[4194304]{0:T(1024)(128)(4,1)S(1)}, s32[]{:S(2)}) async-start(s8[6291456]{0:T(1024)(128)(4,1)} %bitcast.200), calls=%async_computation.14 | async-start | bytes 8388608
  198.6 6.8 %slice-start.7 = ((s8[6291456]{0:T(1024)(128)(4,1)}), s8[2097152]{0:T(1024)(128)(4,1)S(1)}, s32[]{:S(2)}) async-start(s8[6291456]{0:T(1024)(128)(4,1)} %bitcast.200), calls=%async_computation.15 | async-start | bytes 4194304
  209.5 9.3 %copy-start.7 = (bf16[1024,1536]{1,0:T(8,128)(2,1)}, bf16[1024,1536]{1,0:T(8,128)(2,1)S(1)}, u32[]{:S(2)}) copy-start(bf16[1024,1536]{1,0:T(8,128)(2,1)S(1)} %multiply_convert_fusion.3) | copy-start | bytes 9437188
  213.4 8.4 %copy-start.8 = (bf16[1024,1536]{1,0:T(8,128)(2,1)}, bf16[1024,1536]{1,0:T(8,128)(2,1)S(1)}, u32[]{:S(2)}) copy-start(bf16[1024,1536]{1,0:T(8,128)(2,1)S(1)} %multiply_convert_fusion.2) | copy-start | bytes 9437188
  217.6 7.4 %copy-start.10 = (bf16[1024,1536]{1,0:T(8,128)(2,1)}, bf16[1024,1536]{1,0:T(8,128)(2,1)S(1)}, u32[]{:S(2)}) copy-start(bf16[1024,1536]{1,0:T(8,128)(2,1)S(1)} %multiply_convert_fusion.1) | copy-start | bytes 9437188
  221.8 7.2 %slice-start = ((s8[6291456]{0:T(1024)(128)(4,1)}), s8[4194304]{0:T(1024)(128)(4,1)S(1)}, s32[]{:S(2)}) async-start(s8[6291456]{0:T(1024)(128)(4,1)} %bitcast.194), calls=%async_computation.8 | async-start | bytes 8388608
  234.8 11.6 %copy-start.66 = (bf16[1024,128]{1,0:T(8,128)(2,1)S(1)}, bf16[1024,128]{1,0:T(8,128)(2,1)}, u32[]{:S(2)}) copy-start(bf16[1024,128]{1,0:T(8,128)(2,1)} %fusion.119) | copy-start | bytes 786436
  237.9 9.4 %copy-start.67 = (bf16[1024,128]{1,0:T(8,128)(2,1)S(1)}, bf16[1024,128]{1,0:T(8,128)(2,1)}, u32[]{:S(2)}) copy-start(bf16[1024,128]{1,0:T(8,128)(2,1)} %fusion.120) | copy-start | bytes 786436
  237.9 10.2 %copy-start.31 = (bf16[12,1,128,1,128]{4,2,0,3,1:T(8,128)(2,1)S(1)}, bf16[12,1,128,1,128]{4,2,0,3,1:T(8,128)(2,1)}, u32[]{:S(2)}) copy-start(bf16[12,1,128,1,128]{4,2,0,3,1:T(8,128)(2,1)} %get-tuple-element.227) | copy-start | bytes 1179652
  237.9 34.2 %all-to-all-start.6 = ((f32[32,128,1,128]{3,1,2,0:T(8,128)}), f32[32,128,1,128]{3,1,2,0:T(8,128)}, u32[]{:S(2)}, u32[]{:S(2)}) async-start(f32[32,128,1,128]{3,1,2,0:T(8,128)} %bitcast.73), calls=%async_computation.6 | async-start | bytes 4194304 | tf_op jit(solution)/shard_map/all_to_all | solution.py:110
  245.4 6.5 %copy-start.9 = (bf16[1024,1536]{1,0:T(8,128)(2,1)S(1)}, bf16[1024,1536]{1,0:T(8,128)(2,1)}, u32[]{:S(2)}) copy-start(bf16[1024,1536]{1,0:T(8,128)(2,1)} %copy-done.8) | copy-start | bytes 9437188
  245.4 6.5 %copy-start.29 = (bf16[12,1,128,1,128]{4,2,0,3,1:T(8,128)(2,1)S(1)}, bf16[12,1,128,1,128]{4,2,0,3,1:T(8,128)(2,1)}, u32[]{:S(2)}) copy-start(bf16[12,1,128,1,128]{4,2,0,3,1:T(8,128)(2,1)} %get-tuple-element.226) | copy-start | bytes 1179652
  255.7 22.2 %copy-start.58 = (bf16[1024,128]{1,0:T(8,128)(2,1)S(1)}, bf16[1024,128]{1,0:T(8,128)(2,1)}, u32[]{:S(2)}) copy-start(bf16[1024,128]{1,0:T(8,128)(2,1)} %get-tuple-element.267) | copy-start | bytes 786436
  255.7 23.1 %copy-start.62 = (bf16[1024,128]{1,0:T(8,128)(2,1)S(1)}, bf16[1024,128]{1,0:T(8,128)(2,1)}, u32[]{:S(2)}) copy-start(bf16[1024,128]{1,0:T(8,128)(2,1)} %get-tuple-element.269) | copy-start | bytes 786436
  256.7 23.0 %copy-start.63 = (bf16[1024,128]{1,0:T(8,128)(2,1)S(1)}, bf16[1024,128]{1,0:T(8,128)(2,1)}, u32[]{:S(2)}) copy-start(bf16[1024,128]{1,0:T(8,128)(2,1)} %get-tuple-element.271) | copy-start | bytes 786436
  256.7 23.9 %copy-start.64 = (bf16[1024,128]{1,0:T(8,128)(2,1)S(1)}, bf16[1024,128]{1,0:T(8,128)(2,1)}, u32[]{:S(2)}) copy-start(bf16[1024,128]{1,0:T(8,128)(2,1)} %get-tuple-element.273) | copy-start | bytes 786436
  256.7 24.8 %copy-start.65 = (bf16[1024,128]{1,0:T(8,128)(2,1)S(1)}, bf16[1024,128]{1,0:T(8,128)(2,1)}, u32[]{:S(2)}) copy-start(bf16[1024,128]{1,0:T(8,128)(2,1)} %get-tuple-element.275) | copy-start | bytes 786436
  272.0 32.5 %all-to-all-start.5 = ((bf16[32,128,2,128]{3,2,1,0:T(2,128)(2,1)}), bf16[32,128,2,128]{3,2,1,0:T(2,128)(2,1)}, u32[]{:S(2)}, u32[]{:S(2)}) async-start(bf16[32,128,2,128]{3,2,1,0:T(2,128)(2,1)} %bitcast.68), calls=%async_computation.5 | async-start | bytes 4194304 | tf_op jit(solution)/shard_map/all_to_all | solution.py:101
  304.5 32.8 %all-to-all-start.3 = ((bf16[32,128,2,128]{3,2,1,0:T(2,128)(2,1)}), bf16[32,128,2,128]{3,2,1,0:T(2,128)(2,1)}, u32[]{:S(2)}, u32[]{:S(2)}) async-start(bf16[32,128,2,128]{3,2,1,0:T(2,128)(2,1)} %bitcast.45), calls=%async_computation.3 | async-start | bytes 4194304 | tf_op jit(solution)/shard_map/all_to_all | solution.py:94
  (76 other events, 165.7 us)
where the time goes:
time: 349 us; the launch traced here: 343 us
  waiting for transfers between devices  97.4 us (28%)
  matrix products  93.6 us (27%)
  local copies, waits for them, and re-layouts  81.9 us (23%)
  starting transfers between devices  53.3 us (15%)
  other arithmetic  13.5 us (4%)
    dot_general x48, matrix products, contract(): lax.dot_general(left, right, (dims, ((), ())), preferred_element_type=jnp...  93.6 us
    unnamed x252, local copies, waits for them, and re-layouts  39.7 us
    all_to_all x1, waiting for transfers between devices, shards(): lax.all_to_all(queries[None], ('ctx', 'tensor'), split_axis=2, concat_axi...  22 us
    all_to_all x1, waiting for transfers between devices, shards(): lax.all_to_all(attended.reshape(group_size, tok_rows, local_heads, head_w...  17.9 us
    all_to_all x1, waiting for transfers between devices, shards(): lax.all_to_all(grad_block.reshape(group_size, tok_rows, local_heads, head...  16.7 us
    all_to_all x1, waiting for transfers between devices, shards(): lax.all_to_all(key_slots[None], ('ctx', 'tensor'), split_axis=2, concat_a...  14.8 us
    all_to_all x1, waiting for transfers between devices, shards(): lax.all_to_all(key_grad.reshape(group_size, tok_rows, 1, head_width), ('c...  14.4 us
    all_to_all x1, waiting for transfers between devices, shards(): lax.all_to_all(value_slots[None], ('ctx', 'tensor'), split_axis=2, concat...  11.6 us
  transfers between devices with their start and end apart: 8, of which 6 were waited for; matrix products, arithmetic and copies ran while one was open for 36% of the time, Pallas kernels for 0%

commit v1 on v0

v1 whole, which is shorter than its diff:
```python
import functools

import jax
import jax.numpy as jnp
from jax import lax
from jax.experimental import pallas as pl
from jax.experimental.pallas import tpu as pltpu
from jax.sharding import PartitionSpec as P

BLOCK = 128
CHUNK = 256
WINDOW = 2048
LOG2E = 1.4426950408889634
MASKED = -1e30

NT = (((1,), (1,)), ((), ()))
NN = (((1,), (0,)), ((), ()))
TN = (((0,), (0,)), ((), ()))


def dot(a, b, dims):
    return lax.dot_general(a, b, dims, preferred_element_type=jnp.float32)


def attend_block(q, do, bounds, first, last, k_win, v_win, s_scr, dk_acc, dv_acc):
    rows, width = q.shape
    scale = width**-0.5
    low, high = bounds
    key_iota = lax.broadcasted_iota(jnp.int32, (CHUNK, rows), 0)

    def scores(c, top):
        at = pl.ds(pl.multiple_of(c * CHUNK, CHUNK), CHUNK)
        s = dot(k_win[at, :], q, NT)
        pos = key_iota + c * CHUNK
        s = jnp.where((pos >= low) & (pos <= high), s, MASKED)
        s_scr[at, :] = s
        return jnp.maximum(top, jnp.max(s.reshape(CHUNK // 8, 8, rows), axis=0))

    top = lax.fori_loop(first, last, scores, jnp.full((8, rows), MASKED, jnp.float32))
    top = jnp.max(top, axis=0, keepdims=True)

    def forward(c, carry):
        total, att = carry
        at = pl.ds(pl.multiple_of(c * CHUNK, CHUNK), CHUNK)
        e = jnp.exp2((s_scr[at, :] - top) * (scale * LOG2E))
        s_scr[at, :] = e
        total = total + jnp.sum(e.reshape(CHUNK // 8, 8, rows), axis=0)
        att = att + dot(v_win[at, :], e.astype(jnp.bfloat16), TN)
        return total, att

    total, att = lax.fori_loop(
        first, last, forward, (jnp.zeros((8, rows), jnp.float32), jnp.zeros((width, rows), jnp.float32))
    )
    inv = 1.0 / jnp.sum(total, axis=0, keepdims=True)
    att = (att * inv).astype(jnp.bfloat16)
    att_rows = att.astype(jnp.float32).T
    delta = jnp.sum(att.astype(jnp.float32) * do.astype(jnp.float32).T, axis=0, keepdims=True)

    def backward(c, dq):
        at = pl.ds(pl.multiple_of(c * CHUNK, CHUNK), CHUNK)
        k = k_win[at, :]
        p = s_scr[at, :] * inv
        dp = dot(v_win[at, :], do, NT)
        ds = (p * (dp - delta)).astype(jnp.bfloat16)
        dv_acc[at, :] += dot(p.astype(jnp.bfloat16), do, NN)
        dk_acc[at, :] += dot(ds, q, NN)
        return dq + dot(k, ds, TN)

    dq = lax.fori_loop(first, last, backward, jnp.zeros((width, rows), jnp.float32))
    return att_rows.astype(jnp.bfloat16), (dq * scale).T.astype(jnp.bfloat16)


def attend_kernel(meta, q_own, q_got, do_own, do_got, bounds, *refs):
    keys = refs[:10]
    att_own, att_send, dq_own, dq_send = refs[10:14]
    grads = refs[14:22]
    k_win, v_win, s_scr, dk_acc, dv_acc = refs[22:]
    x = meta[0]

    def place(row, half, shift):
        return pl.ds(pl.multiple_of((row * 8 + half * 4 + lax.rem(x + shift, 4)) * BLOCK, BLOCK), BLOCK)

    for row in range(2):
        own, plus, minus, two_a, two_b = keys[row * 5 : row * 5 + 5]
        for half in range(2):
            for ref, shift in ((own, 0), (plus, 3), (minus, 1)):
                k_win[place(row, half, shift), :] = ref[half, 0, 0]
                v_win[place(row, half, shift), :] = ref[half, 1, 0]
            ref = (two_a, two_b)[half]
            k_win[place(row, half, 2), :] = ref[0, 0]
            v_win[place(row, half, 2), :] = ref[1, 0]
    dk_acc[...] = jnp.zeros_like(dk_acc)
    dv_acc[...] = jnp.zeros_like(dv_acc)

    for slot, (q_ref, do_ref, att_ref, dq_ref) in enumerate(
        ((q_own, do_own, att_own, dq_own), (q_got, do_got, att_send, dq_send))
    ):
        shape = (q_ref.shape[0] * q_ref.shape[2], q_ref.shape[3])
        q = q_ref[:, 0].reshape(shape)
        do = do_ref[:, 0].reshape(shape)
        limits = (bounds[2 * slot : 2 * slot + 1, :], bounds[2 * slot + 1 : 2 * slot + 2, :])
        att, dq = attend_block(
            q, do, limits, meta[2 + 2 * slot], meta[3 + 2 * slot], k_win, v_win, s_scr, dk_acc, dv_acc
        )
        att_ref[:, 0] = att.reshape(BLOCK, 8, shape[1])
        dq_ref[:, 0] = dq.reshape(BLOCK, 8, shape[1])

    scale = q_own.shape[3] ** -0.5
    for row in range(2):
        for shift in range(4):
            out = grads[row * 4 + shift]
            for half in range(2):
                at = place(row, half, shift)
                out[half, 0, 0] = (dk_acc[at, :] * scale).astype(jnp.bfloat16)
                out[half, 1, 0] = dv_acc[at, :].astype(jnp.bfloat16)


def attend(meta, q4, q_got, do4, do_got, bounds, keys):
    groups = q_got.shape[1]
    rows = BLOCK * 8
    width = q4.shape[3]
    full = (BLOCK, 1, 8, width)
    own = pl.BlockSpec(full, lambda g, m: (0, g + groups * m[1], 0, 0))
    got = pl.BlockSpec(full, lambda g, m: (0, g, 0, 0))
    pair = pl.BlockSpec((2, 2, 1, BLOCK, width), lambda g, m: (0, 0, g, 0, 0))
    one = pl.BlockSpec((2, 1, BLOCK, width), lambda g, m: (0, g, 0, 0))
    whole = jax.ShapeDtypeStruct(q4.shape, jnp.bfloat16)
    part = jax.ShapeDtypeStruct(q_got.shape, jnp.bfloat16)
    grad = jax.ShapeDtypeStruct((2, 2, groups, BLOCK, width), jnp.bfloat16)
    return pl.pallas_call(
        attend_kernel,
        grid_spec=pltpu.PrefetchScalarGridSpec(
            num_scalar_prefetch=1,
            grid=(groups,),
            in_specs=[own, got, own, got, pl.BlockSpec((4, rows), lambda g, m: (0, 0))]
            + [pair, pair, pair, one, one] * 2,
            out_specs=[own, got, own, got] + [pair] * 8,
            scratch_shapes=[
                pltpu.VMEM((WINDOW, width), jnp.bfloat16),
                pltpu.VMEM((WINDOW, width), jnp.bfloat16),
                pltpu.VMEM((WINDOW, rows), jnp.float32),
                pltpu.VMEM((WINDOW, width), jnp.float32),
                pltpu.VMEM((WINDOW, width), jnp.float32),
            ],
        ),
        out_shape=[whole, part, whole, part] + [grad] * 8,
        compiler_params=pltpu.CompilerParams(vmem_limit_bytes=56 * 1024 * 1024),
        cost_estimate=pl.CostEstimate(flops=10_000_000_000, bytes_accessed=24_000_000, transcendentals=8_000_000),
        name="attend",
    )(meta, q4, q_got, do4, do_got, bounds, *keys)


def shards(queries, key_states, value_states, grad_out, doc_lengths):
    tokens, heads, width = queries.shape
    kv_heads = key_states.shape[1]
    per = heads // kv_heads
    groups = kv_heads // 2
    ctx = lax.axis_index("ctx")
    x = lax.axis_index("tensor")
    y, core = ctx // 2, ctx % 2

    swap = [(i, i ^ 1) for i in range(8)]
    up = [(i, i + 2) for i in range(6)]
    down = [(i + 2, i) for i in range(6)]
    right = [(i, (i + 1) % 4) for i in range(4)]
    left = [(i, (i + 3) % 4) for i in range(4)]

    kv = jnp.stack([key_states, value_states]).transpose(0, 2, 1, 3).reshape(2, 2, groups, tokens, width)
    kv_own = lax.dynamic_index_in_dim(kv, core, 1, keepdims=False)
    kv_send = lax.dynamic_index_in_dim(kv, 1 - core, 1, keepdims=False)
    kv_got = lax.ppermute(kv_send, "ctx", swap)
    row = jnp.stack([jnp.where(core == 0, kv_own, kv_got), jnp.where(core == 0, kv_got, kv_own)])

    def spread(r):
        plus = lax.ppermute(r, "tensor", right)
        minus = lax.ppermute(r, "tensor", left)
        return [r, plus, minus, lax.ppermute(plus[0], "tensor", right), lax.ppermute(minus[1], "tensor", left)]

    before = lax.ppermute(row, "ctx", up)
    here = spread(row)
    earlier = spread(before)

    q4 = queries.reshape(tokens, kv_heads, per, width)
    do4 = grad_out.reshape(tokens, kv_heads, per, width)
    q_got = lax.ppermute(lax.dynamic_slice_in_dim(q4, groups * (1 - core), groups, 1), "ctx", swap)
    do_got = lax.ppermute(lax.dynamic_slice_in_dim(do4, groups * (1 - core), groups, 1), "ctx", swap)

    base = (y - 1) * 1024
    ends = jnp.cumsum(doc_lengths)

    def limits(half):
        pos = y * 1024 + half * 512 + x * tokens + jnp.arange(tokens, dtype=jnp.int32)
        start = jnp.max(jnp.where(ends[None, :] <= pos[:, None], ends[None, :], 0), axis=1)
        return start - base, pos - base

    low0, high0 = limits(core)
    low1, high1 = limits(1 - core)
    bounds = jnp.repeat(jnp.stack([low0, high0, low1, high1]), per, axis=1)
    meta = jnp.stack(
        [x, core, low0[0] // CHUNK, high0[-1] // CHUNK + 1, low1[0] // CHUNK, high1[-1] // CHUNK + 1]
    ).astype(jnp.int32)

    att, att_send, dq, dq_send, *grads = attend(meta, q4, q_got, do4, do_got, bounds, earlier + here)

    def settle(full, send):
        got = lax.ppermute(send, "ctx", swap)
        return lax.dynamic_update_slice_in_dim(full, got, groups * (1 - core), 1).reshape(tokens, heads, width)

    def add(*terms):
        return sum(t.astype(jnp.float32) for t in terms)

    def collect(parts):
        own, plus, two, minus = parts
        two_a = lax.ppermute(two[0], "tensor", right)
        two_b = lax.ppermute(two[1], "tensor", left)
        plus = jnp.stack([add(plus[0], two_a).astype(jnp.bfloat16), plus[1]])
        minus = jnp.stack([minus[0], add(minus[1], two_b).astype(jnp.bfloat16)])
        return add(own, lax.ppermute(plus, "tensor", right), lax.ppermute(minus, "tensor", left))

    back = lax.ppermute(collect(grads[:4]).astype(jnp.bfloat16), "ctx", down)
    both = add(collect(grads[4:]), back).astype(jnp.bfloat16)
    mine = lax.dynamic_index_in_dim(both, core, 0, keepdims=False)
    theirs = lax.ppermute(lax.dynamic_index_in_dim(both, 1 - core, 0, keepdims=False), "ctx", swap)
    kv_grad = jnp.stack([jnp.where(core == 0, mine, theirs), jnp.where(core == 0, theirs, mine)], axis=1)
    kv_grad = kv_grad.reshape(2, kv_heads, tokens, width).transpose(0, 2, 1, 3)
    return settle(att, att_send), settle(dq, dq_send), kv_grad[0], kv_grad[1]


def solution(mesh):
    placed = P(("dp", "ctx", "tensor"), None, None)
    return jax.shard_map(
        shards,
        mesh=mesh,
        in_specs=(placed, placed, placed, placed, P("dp")),
        out_specs=(placed, placed, placed, placed),
        check_vma=False,
    )
```

time: 349 us -> 159 us (0.46); the launches traced: 343 us -> 158 us
  matrix products: 93.6 us -> 0 us
  local copies, waits for them, and re-layouts: 81.9 us -> 12.7 us
  waiting for transfers between devices: 97.4 us -> 31.2 us
  Pallas kernels: 0 us -> 57.6 us
  other arithmetic: 13.5 us -> 2.64 us
  starting transfers between devices: 53.3 us -> 47.5 us
  between operations: 2.84 us -> 6.49 us
    all_to_all x8 -> x0, waiting for transfers between devices: 97.4 us -> none  [the longest x1 22 us: shards(): lax.all_to_all(queries[None], ('ctx', 'tensor'), split_axis=2, concat_axi...]
    dot_general x48 -> x0, matrix products: 93.6 us -> none  [contract(): lax.dot_general(left, right, (dims, ((), ())), preferred_element_type=jnp...]
    pallas_call x0 -> x1, Pallas kernels: none -> 57.6 us  [attend(): pl.pallas_call(attend_kernel, grid_spec=pltpu.PrefetchScalarGridSpec(num_...]
    all_to_all x8 -> x0, starting transfers between devices: 53.3 us -> none  [the longest x1 7.85 us: shards(): lax.all_to_all(key_slots[None], ('ctx', 'tensor'), split_axis=2, concat_a...]
    ppermute x0 -> x24, starting transfers between devices: none -> 47.5 us  [the longest x2 14.6 us: settle(): got = lax.ppermute(send, 'ctx', swap)]
    unnamed x252 -> x45, local copies, waits for them, and re-layouts: 39.7 us -> 2.68 us
    ppermute x0 -> x24, waiting for transfers between devices: none -> 31.2 us  [the longest x1 9.53 us: shards(): before = lax.ppermute(row, 'ctx', up)]
    all_to_all x4 -> x0, local copies, waits for them, and re-layouts: 12 us -> none  [the longest x1 4.01 us: shards(): lax.all_to_all(grad_out[None], ('ctx', 'tensor'), split_axis=2, concat_ax...]
  transfers between devices with their start and end apart: 8 -> 24, of which waited for: 6 -> 8; matrix products, arithmetic and copies ran while one was open for 36% -> 6% of each run, Pallas kernels for 0% -> 0%
where the time goes in v1:
time: 159 us; the launch traced here: 158 us
  Pallas kernels  57.6 us (36%)
  starting transfers between devices  47.5 us (30%)
  waiting for transfers between devices  31.2 us (20%)
  local copies, waits for them, and re-layouts  12.7 us (8%)
  between operations  6.49 us (4%)
  other arithmetic  2.64 us (2%)
    pallas_call x1, Pallas kernels, attend(): pl.pallas_call(attend_kernel, grid_spec=pltpu.PrefetchScalarGridSpec(num_...  57.6 us
    ppermute x2, starting transfers between devices, settle(): got = lax.ppermute(send, 'ctx', swap)  14.6 us
    ppermute x1, waiting for transfers between devices, shards(): before = lax.ppermute(row, 'ctx', up)  9.53 us
    ppermute x1, starting transfers between devices, shards(): lax.ppermute(lax.dynamic_index_in_dim(both, 1 - core, 0, keepdims=False),...  9.11 us
    ppermute x2, waiting for transfers between devices, spread(): minus = lax.ppermute(r, 'tensor', left)  7.52 us
    ppermute x2, waiting for transfers between devices, collect(): lax.ppermute(minus, 'tensor', left)  7.19 us
    ppermute x2, starting transfers between devices, collect(): lax.ppermute(minus, 'tensor', left)  5.12 us
    ppermute x2, starting transfers between devices, spread(): minus = lax.ppermute(r, 'tensor', left)  5.02 us
  transfers between devices with their start and end apart: 24, of which 8 were waited for; matrix products, arithmetic and copies ran while one was open for 6% of the time, Pallas kernels for 0%

profile of v1, /device:TPU:105, one launch (start us, length us, event | category | flops | bytes accessed | tf_op | source)
XLA Modules:
  0.0 158.2 jit_solution(4994222717631661757)
XLA Ops:
  0.7 1.1 pad_maximum_fusion
  1.7 0.2 constant_dynamic-slice_fusion.1
  2.0 0.8 collective-permute-start.2
  2.7 1.3 constant_dynamic-slice_fusion.2
  4.2 1.3 constant_dynamic-slice_fusion.3
  5.5 0.6 collective-permute-start
  6.0 0.2 reduce-window.8
  6.4 3.2 %collective-permute-start.3 = (bf16[2,2,4,128,128]{4,3,2,1,0:T(8,128)(2,1)S(1)}, bf16[2,2,4,128,128]{4,3,2,1,0:T(8,128)(2,1)S(1)}, u32[]{:S(2)}, u32[]{:S(2)}) collective-permute-start(bf16[2,2,4,128,128]{4,3,2,1,0:T(8,128)(2,1)S(1)} %pad_maximum_fusion.1.refs_5_), channel_id=1, source_target_pairs={{0,8},{4,12},{8,16},{12,20},{16,24},{20,28},{1,9},{5,13},{9,17},{1... | collective-permute-start | bytes 1572872 | tf_op jit(solution)/shard_map/ppermute | solution.py:179
  9.7 2.5 %collective-permute-start.9 = (bf16[2,2,4,128,128]{4,3,2,1,0:T(8,128)(2,1)S(1)}, bf16[2,2,4,128,128]{4,3,2,1,0:T(8,128)(2,1)S(1)}, u32[]{:S(2)}, u32[]{:S(2)}) collective-permute-start(bf16[2,2,4,128,128]{4,3,2,1,0:T(8,128)(2,1)S(1)} %pad_maximum_fusion.1.refs_5_), channel_id=1, source_target_pairs={{0,3},{1,0},{2,1},{3,2},{4,7},{5,4},{6,5},{7,6},{8,11},{9,8},{10,9... | collective-permute-start | bytes 1572872 | tf_op jit(solution)/shard_map/ppermute | solution.py:176
  12.2 9.5 %collective-permute-done.3.refs_0_ = bf16[2,2,4,128,128]{4,3,2,1,0:T(8,128)(2,1)S(1)} collective-permute-done((bf16[2,2,4,128,128]{4,3,2,1,0:T(8,128)(2,1)S(1)}, bf16[2,2,4,128,128]{4,3,2,1,0:T(8,128)(2,1)S(1)}, u32[]{:S(2)}, u32[]{:S(2)}) %collective-permute-start.3) | collective-permute-done | bytes 524320 | tf_op jit(solution)/shard_map/ppermute | solution.py:179
  21.8 2.5 %collective-permute-start.5 = (bf16[2,2,4,128,128]{4,3,2,1,0:T(8,128)(2,1)S(1)}, bf16[2,2,4,128,128]{4,3,2,1,0:T(8,128)(2,1)S(1)}, u32[]{:S(2)}, u32[]{:S(2)}) collective-permute-start(bf16[2,2,4,128,128]{4,3,2,1,0:T(8,128)(2,1)S(1)} %collective-permute-done.3.refs_0_), channel_id=1, source_target_pairs={{0,3},{1,0},{2,1},{3,2},{4,7},{5,4},{6,5},{7,6},{8,11},{9,8},{10,9... | collective-permute-start | bytes 1572872 | tf_op jit(solution)/shard_map/ppermute | solution.py:176
  24.4 1.9 %collective-permute-done.8.refs_6_ = bf16[2,2,4,128,128]{4,3,2,1,0:T(8,128)(2,1)S(1)} collective-permute-done((bf16[2,2,4,128,128]{4,3,2,1,0:T(8,128)(2,1)S(1)}, bf16[2,2,4,128,128]{4,3,2,1,0:T(8,128)(2,1)S(1)}, u32[]{:S(2)}, u32[]{:S(2)}) %collective-permute-start.8) | collective-permute-done | bytes 524320 | tf_op jit(solution)/shard_map/ppermute | solution.py:175
  26.3 0.8 collective-permute-start.11
  27.1 7.5 %collective-permute-done.5.refs_2_ = bf16[2,2,4,128,128]{4,3,2,1,0:T(8,128)(2,1)S(1)} collective-permute-done((bf16[2,2,4,128,128]{4,3,2,1,0:T(8,128)(2,1)S(1)}, bf16[2,2,4,128,128]{4,3,2,1,0:T(8,128)(2,1)S(1)}, u32[]{:S(2)}, u32[]{:S(2)}) %collective-permute-start.5) | collective-permute-done | bytes 524320 | tf_op jit(solution)/shard_map/ppermute | solution.py:176
  34.6 0.9 collective-permute-start.10
  35.6 2.2 %collective-permute-done.4.refs_1_ = bf16[2,2,4,128,128]{4,3,2,1,0:T(8,128)(2,1)S(1)} collective-permute-done((bf16[2,2,4,128,128]{4,3,2,1,0:T(8,128)(2,1)S(1)}, bf16[2,2,4,128,128]{4,3,2,1,0:T(8,128)(2,1)S(1)}, u32[]{:S(2)}, u32[]{:S(2)}) %collective-permute-start.4) | collective-permute-done | bytes 524320 | tf_op jit(solution)/shard_map/ppermute | solution.py:175
  37.8 1.0 collective-permute-start.7
  38.9 0.7 slice_bitcast_fusion.5
  39.6 0.7 collective-permute-done.11.refs_9_
  40.3 0.9 collective-permute-start.6
  41.2 0.6 slice.67
  43.7 0.6 slice.69
  47.9 0.8 reshape.111.bounds
  48.7 0.7 stack.85.meta
  49.4 57.6 %attend.1 = (bf16[128,8,8,128]{3,2,1,0:T(8,128)(2,1)}, bf16[128,4,8,128]{3,2,1,0:T(8,128)(2,1)}, bf16[128,8,8,128]{3,2,1,0:T(8,128)(2,1)}, bf16[128,4,8,128]{3,2...) custom-call(s32[6]{0:T(128)} %stack.85.meta, ...), custom_call_target="tpu_custom_call" | custom-call | flops 10000000000 | bytes 24000000 | tf_op jit(solution)/shard_map/attend/pallas_call | solution.py:130
  107.0 1.2 slice_bitcast_fusion.7
  108.3 1.0 slice.76
  109.3 1.0 slice.77
  110.4 1.5 collective-permute-start.14
  112.0 1.2 collective-permute-start.16
  113.2 0.2 collective-permute-start.18
  113.4 4.5 %collective-permute-start.12 = (bf16[128,4,8,128]{3,2,1,0:T(8,128)(2,1)S(1)}, bf16[128,4,8,128]{3,2,1,0:T(8,128)(2,1)S(1)}, u32[]{:S(2)}, u32[]{:S(2)}) collective-permute-start(bf16[128,4,8,128]{3,2,1,0:T(8,128)(2,1)S(1)} %copy-done.17), channel_id=1, source_target_pairs={{0,4},{4,0},{8,12},{12,8},{16,20},{20,16},{24,28},{28,24},{1,5},{5... | collective-permute-start | bytes 3145736 | tf_op jit(solution)/shard_map/ppermute | solution.py:206
  118.1 2.4 %collective-permute-start.21 = (bf16[2,2,4,128,128]{4,3,2,1,0:T(8,128)(2,1)S(1)}, bf16[2,2,4,128,128]{4,3,2,1,0:T(8,128)(2,1)S(1)}, u32[]{:S(2)}, u32[]{:S(2)}) collective-permute-start(bf16[2,2,4,128,128]{4,3,2,1,0:T(8,128)(2,1)S(1)} %pad_maximum_fusion.5), channel_id=1, source_target_pairs={{0,3},{1,0},{2,1},{3,2},{4,7},{5,4},{6,5},{7,6},{8,11},{9,8},{10,9... | collective-permute-start | bytes 1572872 | tf_op jit(solution)/shard_map/ppermute | solution.py:218
  120.5 1.3 collective-permute-done.18
  122.2 2.7 %collective-permute-start.17 = (bf16[2,2,4,128,128]{4,3,2,1,0:T(8,128)(2,1)S(1)}, bf16[2,2,4,128,128]{4,3,2,1,0:T(8,128)(2,1)S(1)}, u32[]{:S(2)}, u32[]{:S(2)}) collective-permute-start(bf16[2,2,4,128,128]{4,3,2,1,0:T(8,128)(2,1)S(1)} %pad_maximum_fusion.3), channel_id=1, source_target_pairs={{0,3},{1,0},{2,1},{3,2},{4,7},{5,4},{6,5},{7,6},{8,11},{9,8},{10,9... | collective-permute-start | bytes 1572872 | tf_op jit(solution)/shard_map/ppermute | solution.py:218
  125.1 7.2 %collective-permute-done.21 = bf16[2,2,4,128,128]{4,3,2,1,0:T(8,128)(2,1)S(1)} collective-permute-done((bf16[2,2,4,128,128]{4,3,2,1,0:T(8,128)(2,1)S(1)}, bf16[2,2,4,128,128]{4,3,2,1,0:T(8,128)(2,1)S(1)}, u32[]{:S(2)}, u32[]{:S(2)}) %collective-permute-start.21) | collective-permute-done | bytes 524320 | tf_op jit(solution)/shard_map/ppermute | solution.py:218
  132.3 0.2 add_convert_fusion.1
  132.6 2.1 %collective-permute-start.22 = (bf16[2,2,4,128,128]{4,3,2,1,0:T(8,128)(2,1)S(1)}, bf16[2,2,4,128,128]{4,3,2,1,0:T(8,128)(2,1)S(1)}, u32[]{:S(2)}, u32[]{:S(2)}) collective-permute-start(bf16[2,2,4,128,128]{4,3,2,1,0:T(8,128)(2,1)S(1)} %add_convert_fusion.1), channel_id=1, source_target_pairs={{8,0},{12,4},{16,8},{20,12},{24,16},{28,20},{9,1},{13,5},{17,9},{2... | collective-permute-start | bytes 1572872 | tf_op jit(solution)/shard_map/ppermute | solution.py:220
  134.6 10.1 %collective-permute-start.13 = (bf16[128,4,8,128]{3,2,1,0:T(8,128)(2,1)S(1)}, bf16[128,4,8,128]{3,2,1,0:T(8,128)(2,1)S(1)}, u32[]{:S(2)}, u32[]{:S(2)}) collective-permute-start(bf16[128,4,8,128]{3,2,1,0:T(8,128)(2,1)S(1)} %copy-done.16), channel_id=1, source_target_pairs={{0,4},{4,0},{8,12},{12,8},{16,20},{20,16},{24,28},{28,24},{1,5},{5... | collective-permute-start | bytes 3145736 | tf_op jit(solution)/shard_map/ppermute | solution.py:206
  144.8 0.3 add_convert_fusion
  145.1 9.1 %collective-permute-start.23 = (bf16[2,4,128,128]{3,2,1,0:T(8,128)(2,1)S(1)}, bf16[2,4,128,128]{3,2,1,0:T(8,128)(2,1)S(1)}, u32[]{:S(2)}, u32[]{:S(2)}) collective-permute-start(bf16[2,4,128,128]{3,2,1,0:T(8,128)(2,1)S(1)} %dynamic-slice_bitcast_fusion), channel_id=1, source_target_pairs={{0,4},{4,0},{8,12},{12,8},{16,20},{20,16},{24,28},{28,24},{1,5},{5... | collective-permute-start | bytes 786440 | tf_op jit(solution)/shard_map/ppermute | solution.py:223
  154.3 0.1 constant_dynamic-update-slice_fusion.1
  154.4 0.2 constant_dynamic-update-slice_fusion
  154.6 0.8 collective-permute-done.23
  155.5 0.2 copy-done.15
  155.8 0.6 copy-done.13
  156.4 0.9 copy.20
  157.3 0.9 copy.19
  (94 shorter events, 1.8 us)
Async XLA Ops:
  2.0 4.3 %collective-permute-start.2 = (bf16[2,4,128,128]{3,2,1,0:T(8,128)(2,1)S(1)}, bf16[2,4,128,128]{3,2,1,0:T(8,128)(2,1)S(1)}, u32[]{:S(2)}, u32[]{:S(2)}) collective-permute-start(bf16[2,4,128,128]{3,2,1,0:T(8,128)(2,1)S(1)} %bitcast.102), channel_id=1, source_target_pairs={{0,4},{4,0},{8,12},{12,8},{16,20},{20,16},{24,28},{28,24},{1,5},{5... | collective-permute-start | bytes 786440 | tf_op jit(solution)/shard_map/ppermute | solution.py:171
  2.7 3.3 %copy-start.20 = (s32[9]{0:T(128)S(1)}, s32[9]{0:T(128)}, u32[]{:S(2)}) copy-start(s32[9]{0:T(128)} %param.9) | copy-start | bytes 112
  4.1 45.3 %collective-permute-start.1 = (bf16[128,4,8,128]{3,2,1,0:T(8,128)(2,1)S(1)}, bf16[128,4,8,128]{3,2,1,0:T(8,128)(2,1)}, u32[]{:S(2)}, u32[]{:S(2)}) collective-permute-start(bf16[128,4,8,128]{3,2,1,0:T(8,128)(2,1)S(1)} %constant_dynamic-slice_fusion.2), channel_id=1, source_target_pairs={{0,4},{4,0},{8,12},{12,8},{16,20},{20,16},{24,28},{28,24},{1,5},{5... | collective-permute-start | bytes 3145736 | tf_op jit(solution)/shard_map/ppermute | solution.py:186
  5.5 43.9 %collective-permute-start = (bf16[128,4,8,128]{3,2,1,0:T(8,128)(2,1)S(1)}, bf16[128,4,8,128]{3,2,1,0:T(8,128)(2,1)}, u32[]{:S(2)}, u32[]{:S(2)}) collective-permute-start(bf16[128,4,8,128]{3,2,1,0:T(8,128)(2,1)S(1)} %constant_dynamic-slice_fusion.3), channel_id=1, source_target_pairs={{0,4},{4,0},{8,12},{12,8},{16,20},{20,16},{24,28},{28,24},{1,5},{5... | collective-permute-start | bytes 3145736 | tf_op jit(solution)/shard_map/ppermute | solution.py:185
  6.4 43.0 %copy-start.5 = (bf16[2,2,4,128,128]{4,3,2,1,0:T(8,128)(2,1)}, bf16[2,2,4,128,128]{4,3,2,1,0:T(8,128)(2,1)S(1)}, u32[]{:S(2)}) copy-start(bf16[2,2,4,128,128]{4,3,2,1,0:T(8,128)(2,1)S(1)} %pad_maximum_fusion.1.refs_5_) | copy-start | bytes 1572868
  6.4 15.4 %collective-permute-start.3 = (bf16[2,2,4,128,128]{4,3,2,1,0:T(8,128)(2,1)S(1)}, bf16[2,2,4,128,128]{4,3,2,1,0:T(8,128)(2,1)S(1)}, u32[]{:S(2)}, u32[]{:S(2)}) collective-permute-start(bf16[2,2,4,128,128]{4,3,2,1,0:T(8,128)(2,1)S(1)} %pad_maximum_fusion.1.refs_5_), channel_id=1, source_target_pairs={{0,8},{4,12},{8,16},{12,20},{16,24},{20,28},{1,9},{5,13},{9,17},{1... | collective-permute-start | bytes 1572872 | tf_op jit(solution)/shard_map/ppermute | solution.py:179
  9.7 14.6 %collective-permute-start.9 = (bf16[2,2,4,128,128]{4,3,2,1,0:T(8,128)(2,1)S(1)}, bf16[2,2,4,128,128]{4,3,2,1,0:T(8,128)(2,1)S(1)}, u32[]{:S(2)}, u32[]{:S(2)}) collective-permute-start(bf16[2,2,4,128,128]{4,3,2,1,0:T(8,128)(2,1)S(1)} %pad_maximum_fusion.1.refs_5_), channel_id=1, source_target_pairs={{0,3},{1,0},{2,1},{3,2},{4,7},{5,4},{6,5},{7,6},{8,11},{9,8},{10,9... | collective-permute-start | bytes 1572872 | tf_op jit(solution)/shard_map/ppermute | solution.py:176
  12.2 14.1 %collective-permute-start.8 = (bf16[2,2,4,128,128]{4,3,2,1,0:T(8,128)(2,1)S(1)}, bf16[2,2,4,128,128]{4,3,2,1,0:T(8,128)(2,1)S(1)}, u32[]{:S(2)}, u32[]{:S(2)}) collective-permute-start(bf16[2,2,4,128,128]{4,3,2,1,0:T(8,128)(2,1)S(1)} %pad_maximum_fusion.1.refs_5_), channel_id=1, source_target_pairs={{0,1},{1,2},{2,3},{3,0},{4,5},{5,6},{6,7},{7,4},{8,9},{9,10},{10,1... | collective-permute-start | bytes 1572872 | tf_op jit(solution)/shard_map/ppermute | solution.py:175
  21.8 20.0 %copy-start.18 = (bf16[2,2,4,128,128]{4,3,2,1,0:T(8,128)(2,1)}, bf16[2,2,4,128,128]{4,3,2,1,0:T(8,128)(2,1)S(1)}, u32[]{:S(2)}) copy-start(bf16[2,2,4,128,128]{4,3,2,1,0:T(8,128)(2,1)S(1)} %collective-permute-done.3.refs_0_) | copy-start | bytes 1572868
  21.8 12.9 %collective-permute-start.5 = (bf16[2,2,4,128,128]{4,3,2,1,0:T(8,128)(2,1)S(1)}, bf16[2,2,4,128,128]{4,3,2,1,0:T(8,128)(2,1)S(1)}, u32[]{:S(2)}, u32[]{:S(2)}) collective-permute-start(bf16[2,2,4,128,128]{4,3,2,1,0:T(8,128)(2,1)S(1)} %collective-permute-done.3.refs_0_), channel_id=1, source_target_pairs={{0,3},{1,0},{2,1},{3,2},{4,7},{5,4},{6,5},{7,6},{8,11},{9,8},{10,9... | collective-permute-start | bytes 1572872 | tf_op jit(solution)/shard_map/ppermute | solution.py:176
  24.2 16.0 %copy-start.8 = (bf16[2,2,4,128,128]{4,3,2,1,0:T(8,128)(2,1)}, bf16[2,2,4,128,128]{4,3,2,1,0:T(8,128)(2,1)S(1)}, u32[]{:S(2)}) copy-start(bf16[2,2,4,128,128]{4,3,2,1,0:T(8,128)(2,1)S(1)} %collective-permute-done.9.refs_7_) | copy-start | bytes 1572868
  24.3 13.6 %collective-permute-start.4 = (bf16[2,2,4,128,128]{4,3,2,1,0:T(8,128)(2,1)S(1)}, bf16[2,2,4,128,128]{4,3,2,1,0:T(8,128)(2,1)S(1)}, u32[]{:S(2)}, u32[]{:S(2)}) collective-permute-start(bf16[2,2,4,128,128]{4,3,2,1,0:T(8,128)(2,1)S(1)} %collective-permute-done.3.refs_0_), channel_id=1, source_target_pairs={{0,1},{1,2},{2,3},{3,0},{4,5},{5,6},{6,7},{7,4},{8,9},{9,10},{10,1... | collective-permute-start | bytes 1572872 | tf_op jit(solution)/shard_map/ppermute | solution.py:175
  26.3 14.9 %copy-start.9 = (bf16[2,2,4,128,128]{4,3,2,1,0:T(8,128)(2,1)}, bf16[2,2,4,128,128]{4,3,2,1,0:T(8,128)(2,1)S(1)}, u32[]{:S(2)}) copy-start(bf16[2,2,4,128,128]{4,3,2,1,0:T(8,128)(2,1)S(1)} %collective-permute-done.8.refs_6_) | copy-start | bytes 1572868
  26.3 14.0 %collective-permute-start.11 = (bf16[2,4,128,128]{3,2,1,0:T(8,128)(2,1)S(1)}, bf16[2,4,128,128]{3,2,1,0:T(8,128)(2,1)S(1)}, u32[]{:S(2)}, u32[]{:S(2)}) collective-permute-start(bf16[2,4,128,128]{3,2,1,0:T(8,128)(2,1)S(1)} %slice_bitcast_fusion.2), channel_id=1, source_target_pairs={{0,3},{1,0},{2,1},{3,2},{4,7},{5,4},{6,5},{7,6},{8,11},{9,8},{10,9... | collective-permute-start | bytes 786440 | tf_op jit(solution)/shard_map/ppermute | solution.py:177
  34.6 6.6 %copy-start.10 = (bf16[2,2,4,128,128]{4,3,2,1,0:T(8,128)(2,1)}, bf16[2,2,4,128,128]{4,3,2,1,0:T(8,128)(2,1)S(1)}, u32[]{:S(2)}) copy-start(bf16[2,2,4,128,128]{4,3,2,1,0:T(8,128)(2,1)S(1)} %collective-permute-done.5.refs_2_) | copy-start | bytes 1572868
  34.6 14.7 %collective-permute-start.10 = (bf16[2,4,128,128]{3,2,1,0:T(8,128)(2,1)S(1)}, bf16[2,4,128,128]{3,2,1,0:T(8,128)(2,1)}, u32[]{:S(2)}, u32[]{:S(2)}) collective-permute-start(bf16[2,4,128,128]{3,2,1,0:T(8,128)(2,1)S(1)} %slice_bitcast_fusion.3), channel_id=1, source_target_pairs={{0,1},{1,2},{2,3},{3,0},{4,5},{5,6},{6,7},{7,4},{8,9},{9,10},{10,1... | collective-permute-start | bytes 786440 | tf_op jit(solution)/shard_map/ppermute | solution.py:177
  37.8 3.4 %copy-start.11 = (bf16[2,2,4,128,128]{4,3,2,1,0:T(8,128)(2,1)}, bf16[2,2,4,128,128]{4,3,2,1,0:T(8,128)(2,1)S(1)}, u32[]{:S(2)}) copy-start(bf16[2,2,4,128,128]{4,3,2,1,0:T(8,128)(2,1)S(1)} %collective-permute-done.4.refs_1_) | copy-start | bytes 1572868
  37.8 11.5 %collective-permute-start.7 = (bf16[2,4,128,128]{3,2,1,0:T(8,128)(2,1)S(1)}, bf16[2,4,128,128]{3,2,1,0:T(8,128)(2,1)}, u32[]{:S(2)}, u32[]{:S(2)}) collective-permute-start(bf16[2,4,128,128]{3,2,1,0:T(8,128)(2,1)S(1)} %slice_bitcast_fusion.4), channel_id=1, source_target_pairs={{0,3},{1,0},{2,1},{3,2},{4,7},{5,4},{6,5},{7,6},{8,11},{9,8},{10,9... | collective-permute-start | bytes 786440 | tf_op jit(solution)/shard_map/ppermute | solution.py:177
  40.3 1.5 copy-start.19
  40.3 9.1 %collective-permute-start.6 = (bf16[2,4,128,128]{3,2,1,0:T(8,128)(2,1)}, bf16[2,4,128,128]{3,2,1,0:T(8,128)(2,1)}, u32[]{:S(2)}, u32[]{:S(2)}) collective-permute-start(bf16[2,4,128,128]{3,2,1,0:T(8,128)(2,1)} %slice_bitcast_fusion.5), channel_id=1, source_target_pairs={{0,1},{1,2},{2,3},{3,0},{4,5},{5,6},{6,7},{7,4},{8,9},{9,10},{10,1... | collective-permute-start | bytes 786440 | tf_op jit(solution)/shard_map/ppermute | solution.py:177
  107.0 3.3 %copy-start.3 = (bf16[2,2,4,128,128]{4,3,2,1,0:T(8,128)(2,1)S(1)}, bf16[2,2,4,128,128]{4,3,2,1,0:T(8,128)(2,1)}, u32[]{:S(2)}) copy-start(bf16[2,2,4,128,128]{4,3,2,1,0:T(8,128)(2,1)} %get-tuple-element.25) | copy-start | bytes 1572868
  107.0 3.3 %copy-start.4 = (bf16[2,2,4,128,128]{4,3,2,1,0:T(8,128)(2,1)S(1)}, bf16[2,2,4,128,128]{4,3,2,1,0:T(8,128)(2,1)}, u32[]{:S(2)}) copy-start(bf16[2,2,4,128,128]{4,3,2,1,0:T(8,128)(2,1)} %get-tuple-element.27) | copy-start | bytes 1572868
  107.0 3.3 %copy-start.6 = (bf16[2,2,4,128,128]{4,3,2,1,0:T(8,128)(2,1)S(1)}, bf16[2,2,4,128,128]{4,3,2,1,0:T(8,128)(2,1)}, u32[]{:S(2)}) copy-start(bf16[2,2,4,128,128]{4,3,2,1,0:T(8,128)(2,1)} %get-tuple-element.22) | copy-start | bytes 1572868
  107.0 6.4 %copy-start.17 = (bf16[128,4,8,128]{3,2,1,0:T(8,128)(2,1)S(1)}, bf16[128,4,8,128]{3,2,1,0:T(8,128)(2,1)}, u32[]{:S(2)}) copy-start(bf16[128,4,8,128]{3,2,1,0:T(8,128)(2,1)} %get-tuple-element.17) | copy-start | bytes 3145732
  108.3 9.6 %collective-permute-start.20 = (bf16[2,4,128,128]{3,2,1,0:T(8,128)(2,1)S(1)}, bf16[2,4,128,128]{3,2,1,0:T(8,128)(2,1)S(1)}, u32[]{:S(2)}, u32[]{:S(2)}) collective-permute-start(bf16[2,4,128,128]{3,2,1,0:T(8,128)(2,1)S(1)} %get-tuple-element.45), channel_id=1, source_target_pairs={{0,3},{1,0},{2,1},{3,2},{4,7},{5,4},{6,5},{7,6},{8,11},{9,8},{10,9... | collective-permute-start | bytes 786440 | tf_op jit(solution)/shard_map/ppermute | solution.py:215
  110.4 11.6 %copy-start.2 = (bf16[2,2,4,128,128]{4,3,2,1,0:T(8,128)(2,1)S(1)}, bf16[2,2,4,128,128]{4,3,2,1,0:T(8,128)(2,1)}, u32[]{:S(2)}) copy-start(bf16[2,2,4,128,128]{4,3,2,1,0:T(8,128)(2,1)} %get-tuple-element.23) | copy-start | bytes 1572868
  110.4 14.5 %collective-permute-start.14 = (bf16[2,4,128,128]{3,2,1,0:T(8,128)(2,1)S(1)}, bf16[2,4,128,128]{3,2,1,0:T(8,128)(2,1)S(1)}, u32[]{:S(2)}, u32[]{:S(2)}) collective-permute-start(bf16[2,4,128,128]{3,2,1,0:T(8,128)(2,1)S(1)} %get-tuple-element.42), channel_id=1, source_target_pairs={{0,1},{1,2},{2,3},{3,0},{4,5},{5,6},{6,7},{7,4},{8,9},{9,10},{10,1... | collective-permute-start | bytes 786440 | tf_op jit(solution)/shard_map/ppermute | solution.py:214
  112.0 10.0 %collective-permute-start.16 = (bf16[2,4,128,128]{3,2,1,0:T(8,128)(2,1)S(1)}, bf16[2,4,128,128]{3,2,1,0:T(8,128)(2,1)S(1)}, u32[]{:S(2)}, u32[]{:S(2)}) collective-permute-start(bf16[2,4,128,128]{3,2,1,0:T(8,128)(2,1)S(1)} %get-tuple-element.43), channel_id=1, source_target_pairs={{0,3},{1,0},{2,1},{3,2},{4,7},{5,4},{6,5},{7,6},{8,11},{9,8},{10,9... | collective-permute-start | bytes 786440 | tf_op jit(solution)/shard_map/ppermute | solution.py:215
  113.2 8.6 %collective-permute-start.18 = (bf16[2,4,128,128]{3,2,1,0:T(8,128)(2,1)S(1)}, bf16[2,4,128,128]{3,2,1,0:T(8,128)(2,1)S(1)}, u32[]{:S(2)}, u32[]{:S(2)}) collective-permute-start(bf16[2,4,128,128]{3,2,1,0:T(8,128)(2,1)S(1)} %get-tuple-element.44), channel_id=1, source_target_pairs={{0,1},{1,2},{2,3},{3,0},{4,5},{5,6},{6,7},{7,4},{8,9},{9,10},{10,1... | collective-permute-start | bytes 786440 | tf_op jit(solution)/shard_map/ppermute | solution.py:214
  113.4 40.8 %collective-permute-start.12 = (bf16[128,4,8,128]{3,2,1,0:T(8,128)(2,1)S(1)}, bf16[128,4,8,128]{3,2,1,0:T(8,128)(2,1)S(1)}, u32[]{:S(2)}, u32[]{:S(2)}) collective-permute-start(bf16[128,4,8,128]{3,2,1,0:T(8,128)(2,1)S(1)} %copy-done.17), channel_id=1, source_target_pairs={{0,4},{4,0},{8,12},{12,8},{16,20},{20,16},{24,28},{28,24},{1,5},{5... | collective-permute-start | bytes 3145736 | tf_op jit(solution)/shard_map/ppermute | solution.py:206
  118.0 6.9 %copy-start.1 = (bf16[2,2,4,128,128]{4,3,2,1,0:T(8,128)(2,1)S(1)}, bf16[2,2,4,128,128]{4,3,2,1,0:T(8,128)(2,1)}, u32[]{:S(2)}) copy-start(bf16[2,2,4,128,128]{4,3,2,1,0:T(8,128)(2,1)} %get-tuple-element.21) | copy-start | bytes 1572868
  118.1 14.3 %collective-permute-start.21 = (bf16[2,2,4,128,128]{4,3,2,1,0:T(8,128)(2,1)S(1)}, bf16[2,2,4,128,128]{4,3,2,1,0:T(8,128)(2,1)S(1)}, u32[]{:S(2)}, u32[]{:S(2)}) collective-permute-start(bf16[2,2,4,128,128]{4,3,2,1,0:T(8,128)(2,1)S(1)} %pad_maximum_fusion.5), channel_id=1, source_target_pairs={{0,3},{1,0},{2,1},{3,2},{4,7},{5,4},{6,5},{7,6},{8,11},{9,8},{10,9... | collective-permute-start | bytes 1572872 | tf_op jit(solution)/shard_map/ppermute | solution.py:218
  121.9 10.4 %copy-start.7 = (bf16[2,2,4,128,128]{4,3,2,1,0:T(8,128)(2,1)S(1)}, bf16[2,2,4,128,128]{4,3,2,1,0:T(8,128)(2,1)}, u32[]{:S(2)}) copy-start(bf16[2,2,4,128,128]{4,3,2,1,0:T(8,128)(2,1)} %get-tuple-element.24) | copy-start | bytes 1572868
  121.9 10.4 %collective-permute-start.19 = (bf16[2,2,4,128,128]{4,3,2,1,0:T(8,128)(2,1)S(1)}, bf16[2,2,4,128,128]{4,3,2,1,0:T(8,128)(2,1)S(1)}, u32[]{:S(2)}, u32[]{:S(2)}) collective-permute-start(bf16[2,2,4,128,128]{4,3,2,1,0:T(8,128)(2,1)S(1)} %pad_maximum_fusion.4), channel_id=1, source_target_pairs={{0,1},{1,2},{2,3},{3,0},{4,5},{5,6},{6,7},{7,4},{8,9},{9,10},{10,1... | collective-permute-start | bytes 1572872 | tf_op jit(solution)/shard_map/ppermute | solution.py:218
  122.2 12.5 %copy-start.16 = (bf16[128,4,8,128]{3,2,1,0:T(8,128)(2,1)S(1)}, bf16[128,4,8,128]{3,2,1,0:T(8,128)(2,1)}, u32[]{:S(2)}) copy-start(bf16[128,4,8,128]{3,2,1,0:T(8,128)(2,1)} %get-tuple-element.19) | copy-start | bytes 3145732
  122.2 22.6 %copy-start = (bf16[2,2,4,128,128]{4,3,2,1,0:T(8,128)(2,1)S(1)}, bf16[2,2,4,128,128]{4,3,2,1,0:T(8,128)(2,1)}, u32[]{:S(2)}) copy-start(bf16[2,2,4,128,128]{4,3,2,1,0:T(8,128)(2,1)} %get-tuple-element.20) | copy-start | bytes 1572868
  122.2 22.6 %collective-permute-start.17 = (bf16[2,2,4,128,128]{4,3,2,1,0:T(8,128)(2,1)S(1)}, bf16[2,2,4,128,128]{4,3,2,1,0:T(8,128)(2,1)S(1)}, u32[]{:S(2)}, u32[]{:S(2)}) collective-permute-start(bf16[2,2,4,128,128]{4,3,2,1,0:T(8,128)(2,1)S(1)} %pad_maximum_fusion.3), channel_id=1, source_target_pairs={{0,3},{1,0},{2,1},{3,2},{4,7},{5,4},{6,5},{7,6},{8,11},{9,8},{10,9... | collective-permute-start | bytes 1572872 | tf_op jit(solution)/shard_map/ppermute | solution.py:218
  125.0 19.7 %collective-permute-start.15 = (bf16[2,2,4,128,128]{4,3,2,1,0:T(8,128)(2,1)S(1)}, bf16[2,2,4,128,128]{4,3,2,1,0:T(8,128)(2,1)S(1)}, u32[]{:S(2)}, u32[]{:S(2)}) collective-permute-start(bf16[2,2,4,128,128]{4,3,2,1,0:T(8,128)(2,1)S(1)} %pad_maximum_fusion.2), channel_id=1, source_target_pairs={{0,1},{1,2},{2,3},{3,0},{4,5},{5,6},{6,7},{7,4},{8,9},{9,10},{10,1... | collective-permute-start | bytes 1572872 | tf_op jit(solution)/shard_map/ppermute | solution.py:218
  132.6 21.7 %copy-start.14 = (bf16[128,8,8,128]{3,2,1,0:T(8,128)(2,1)S(1)}, bf16[128,8,8,128]{3,2,1,0:T(8,128)(2,1)}, u32[]{:S(2)}) copy-start(bf16[128,8,8,128]{3,2,1,0:T(8,128)(2,1)} %get-tuple-element.16) | copy-start | bytes 6291460
  132.6 12.2 %collective-permute-start.22 = (bf16[2,2,4,128,128]{4,3,2,1,0:T(8,128)(2,1)S(1)}, bf16[2,2,4,128,128]{4,3,2,1,0:T(8,128)(2,1)S(1)}, u32[]{:S(2)}, u32[]{:S(2)}) collective-permute-start(bf16[2,2,4,128,128]{4,3,2,1,0:T(8,128)(2,1)S(1)} %add_convert_fusion.1), channel_id=1, source_target_pairs={{8,0},{12,4},{16,8},{20,12},{24,16},{28,20},{9,1},{13,5},{17,9},{2... | collective-permute-start | bytes 1572872 | tf_op jit(solution)/shard_map/ppermute | solution.py:220
  134.6 19.8 %collective-permute-start.13 = (bf16[128,4,8,128]{3,2,1,0:T(8,128)(2,1)S(1)}, bf16[128,4,8,128]{3,2,1,0:T(8,128)(2,1)S(1)}, u32[]{:S(2)}, u32[]{:S(2)}) collective-permute-start(bf16[128,4,8,128]{3,2,1,0:T(8,128)(2,1)S(1)} %copy-done.16), channel_id=1, source_target_pairs={{0,4},{4,0},{8,12},{12,8},{16,20},{20,16},{24,28},{28,24},{1,5},{5... | collective-permute-start | bytes 3145736 | tf_op jit(solution)/shard_map/ppermute | solution.py:206
  144.8 9.7 %copy-start.12 = (bf16[128,8,8,128]{3,2,1,0:T(8,128)(2,1)S(1)}, bf16[128,8,8,128]{3,2,1,0:T(8,128)(2,1)}, u32[]{:S(2)}) copy-start(bf16[128,8,8,128]{3,2,1,0:T(8,128)(2,1)} %get-tuple-element.18) | copy-start | bytes 6291460
  145.1 10.3 %collective-permute-start.23 = (bf16[2,4,128,128]{3,2,1,0:T(8,128)(2,1)S(1)}, bf16[2,4,128,128]{3,2,1,0:T(8,128)(2,1)S(1)}, u32[]{:S(2)}, u32[]{:S(2)}) collective-permute-start(bf16[2,4,128,128]{3,2,1,0:T(8,128)(2,1)S(1)} %dynamic-slice_bitcast_fusion), channel_id=1, source_target_pairs={{0,4},{4,0},{8,12},{12,8},{16,20},{20,16},{24,28},{28,24},{1,5},{5... | collective-permute-start | bytes 786440 | tf_op jit(solution)/shard_map/ppermute | solution.py:223
  154.4 1.3 copy-start.15
  154.6 1.8 %copy-start.13 = (bf16[128,8,8,128]{3,2,1,0:T(8,128)(2,1)}, bf16[128,8,8,128]{3,2,1,0:T(8,128)(2,1)S(1)}, u32[]{:S(2)}) copy-start(bf16[128,8,8,128]{3,2,1,0:T(8,128)(2,1)S(1)} %constant_dynamic-update-slice_fusion) | copy-start | bytes 6291460
